TPU v7x, 32 devices: a whole 2x2x4 slice. The times are simulated.
32 devices in a mesh: member: 8 (over y, x, core), tile: 4 (over z).
Axes of the slice: x: 2, y: 2, z: 4, core: 2. Of those that a mesh axis runs over, the one named last changes fastest.
Arguments:
- perturbations: bfloat16 [64, 2, 5, 8, 8, 512], P('member', None, None, None, None, 'tile'), may hold values from -6 to 6
- gradient_store: float32 [2, 5, 8, 8, 512], P(None, None, None, 'member', 'tile'), may hold values from -6 to 6
- diffusivity: float32 [8, 8, 512], P(None, None, 'tile'), may hold values from 0.2 to 0.4
- slab_owner: int32 [8], replicated, may hold values from 0 to 7, each once
Outputs:
- increment_store: float32 [2, 5, 8, 8, 512], P(None, None, None, 'member', 'tile')
Inputs may be any that keep to these rules, and one draw needn't show every extreme that they name: `slab_owner`: each member index holds exactly one slab.
All inputs are finite; a program needn't handle non-finite values.
Results may differ from a plain program's by a relative error of at most 0.0003.
Values sent between devices are 32-bit elements; how exact they have to be, the bound alone decides.
No kernel may reach another device: no remote copies, remote signals or barrier semaphores. Data moves between devices by JAX's collectives and lax.ppermute only.
A program may use at most 128 MiB of HBM per device.

v0:
```python
import math

import jax
import jax.numpy as jnp
from jax import lax
from jax.experimental import pallas as pl
from jax.experimental.pallas import tpu as pltpu
from jax.sharding import PartitionSpec as P

SWEEPS = 10
SLOTS = 4
ANCHOR_WORK = 10**10
VMEM_LIMIT = 16 * 1024 * 1024


def lane_roll(value, shift):
    shift = shift % value.shape[-1]
    return value if shift == 0 else pltpu.roll(value, shift, 1)


def lane_index(shape):
    return lax.broadcasted_iota(jnp.int32, shape, 1)


def pick(values, which):
    result = values[0]
    for index in range(1, len(values)):
        result = jnp.where(which == index, values[index], result)
    return result


def spread(row, rows=8):
    return jnp.broadcast_to(row, (rows, row.shape[-1]))


def pack_sizes(rows):
    folded_rows = rows // 2
    slots = min(SLOTS, folded_rows)
    return folded_rows, slots, folded_rows // slots


def own_strip(near, far):
    lanes = near.shape[-1]
    half, part = lanes // 2, lanes // 4
    lane = lane_index(near.shape)
    far = lane_roll(far, half)
    start = half - SWEEPS
    first = jnp.where((lane >= start) & (lane < start + part), far, near)
    start = half + SWEEPS - part
    second = jnp.where((lane >= start) & (lane < start + part), far, near)
    return jnp.where(
        lane % half < part,
        lane_roll(first, SWEEPS),
        lane_roll(second, half - SWEEPS),
    )


def strip_ends(strip):
    lanes = strip.shape[-1]
    half, part = lanes // 2, lanes // 4
    lane = lane_index(strip.shape)
    ends = jnp.where(
        lane % half < part, lane_roll(strip, -SWEEPS), lane_roll(strip, half + SWEEPS)
    )
    return ends, lane_roll(ends, half)


def packed_edges(strips):
    lanes = strips[0].shape[-1]
    half = lanes // 2
    block = half // len(strips)
    slot = (lane_index(strips[0].shape) % half) // block
    to_right = pick([lane_roll(s, i * block) for i, s in enumerate(strips)], slot)
    to_left = pick([lane_roll(s, (i + 1) * block - half) for i, s in enumerate(strips)], slot)
    return to_right, to_left


def joined_strip(own, from_left, from_right, slot, block):
    lanes = own.shape[-1]
    half = lanes // 2
    place = lane_index(own.shape) % half
    left = lane_roll(from_left, -slot * block)
    right = lane_roll(from_right, half - (slot + 1) * block)
    return jnp.where(place < SWEEPS, left, jnp.where(place >= half - SWEEPS, right, own))


def total(terms):
    terms = list(terms)
    while len(terms) > 1:
        terms = [
            terms[i] + terms[i + 1] if i + 1 < len(terms) else terms[i]
            for i in range(0, len(terms), 2)
        ]
    return terms[0]


def around(planes, level, row, folded):
    levels, rows = len(planes), len(planes[level])
    here = planes[level][row]
    terms = [lane_roll(here, 1), lane_roll(here, -1)]
    if row > 0:
        terms.append(planes[level][row - 1])
    if row < rows - 1:
        terms.append(planes[level][row + 1])
    elif folded:
        terms.append(lane_roll(here, here.shape[-1] // 2))
    if level > 0:
        terms.append(planes[level - 1][row])
    if level < levels - 1:
        terms.append(planes[level + 1][row])
    return total(terms)


def sweep(source, target, keep_at, square_at, folded):
    levels, rows = source.shape[0], source.shape[1]
    planes = [[source[level, row] for row in range(rows)] for level in range(levels)]
    for level in range(levels):
        for row in range(rows):
            target[level, row] = keep_at(level, row) * planes[level][row] + square_at(
                level, row
            ) * around(planes, level, row, folded)


def level_rows(coeff_ref, row):
    levels = coeff_ref.shape[0]
    return jnp.concatenate([coeff_ref[level, pl.ds(row, 1), :] for level in range(levels)], axis=0)


def own_coefficient_strip(coeff_ref, row):
    rows = coeff_ref.shape[1]
    return own_strip(level_rows(coeff_ref, row), level_rows(coeff_ref, rows - 1 - row))


def anchor_kernel(out_ref):
    out_ref[...] = jnp.zeros_like(out_ref)


def weigh_kernel(
    owner_ref,
    gathered_ref,
    pert_ref,
    coeff_ref,
    anchor_ref,
    field_ref,
    strip_ref,
    right_ref,
    left_ref,
    grad_ref,
):
    members, terms, levels, rows, lanes = pert_ref.shape
    slab_rows = gathered_ref.shape[2]
    folded_rows, slots, packs = pack_sizes(rows)
    for pack in range(packs):
        strips = [own_coefficient_strip(coeff_ref, pack * slots + slot) for slot in range(slots)]
        for ref, packed in zip((right_ref, left_ref), packed_edges(strips)):
            ref[pl.ds(levels * (packs * members + pack), levels), :] = packed

    for slab in range(rows // slab_rows):
        owner = owner_ref[slab]
        for inner in range(slab_rows):
            row = slab * slab_rows + inner
            coeff = level_rows(coeff_ref, row)
            for term in range(terms):
                grad_ref[pl.ds(term * levels * rows + row, levels, stride=rows), :] = (
                    coeff * gathered_ref[owner, term, inner]
                )

    def weigh_level(level, carry):
        base = level * rows
        gradients = [
            grad_ref[pl.ds(pl.multiple_of(term * levels * rows + base, rows), rows), :]
            for term in range(terms)
        ]
        for member in range(members):
            field_ref[pl.ds(base * members + member, rows, stride=members), :] = total(
                pert_ref[member, term, level].astype(jnp.float32) * gradients[term]
                for term in range(terms)
            )
        return carry

    lax.fori_loop(0, levels, weigh_level, 0)

    def field_at(level, row):
        return field_ref[pl.ds((level * rows + row) * members, members), :]

    for level in range(levels):
        for pack in range(packs):
            strips = []
            for slot in range(slots):
                row = pack * slots + slot
                strip = own_strip(field_at(level, row), field_at(level, rows - 1 - row))
                strip_ref[level, row] = strip
                strips.append(strip)
            place = level * packs + pack
            for ref, packed in zip((right_ref, left_ref), packed_edges(strips)):
                ref[pl.ds(place * members, members), :] = packed


def interior_kernel(
    field_ref,
    coeff_ref,
    out_ref,
    coeff_strip_ref,
    other_ref,
    keep_ref,
    square_ref,
    inverse_ref,
):
    levels, rows, members, lanes = field_ref.shape
    folded_rows = rows // 2
    row_index = lax.broadcasted_iota(jnp.int32, (rows, lanes), 0)
    for level in range(levels):
        here = coeff_ref[level]
        terms = [
            lane_roll(here, 1),
            lane_roll(here, -1),
            jnp.where(row_index > 0, pltpu.roll(here, 1, 0), 0.0),
            jnp.where(row_index < rows - 1, pltpu.roll(here, rows - 1, 0), 0.0),
        ]
        if level > 0:
            terms.append(coeff_ref[level - 1])
        if level < levels - 1:
            terms.append(coeff_ref[level + 1])
        keep_ref[level] = 1.0 - here * total(terms)
        square_ref[level] = here * here
        inverse_ref[level] = 1.0 / here
    def keep_at(level, row):
        return keep_ref[level, pl.ds(row, 1), :]

    def square_at(level, row):
        return square_ref[level, pl.ds(row, 1), :]

    sweep(field_ref, other_ref, keep_at, square_at, False)
    sweep(other_ref, out_ref, keep_at, square_at, False)

    def pair(index, carry):
        sweep(out_ref, other_ref, keep_at, square_at, False)
        sweep(other_ref, out_ref, keep_at, square_at, False)
        return carry

    lax.fori_loop(0, SWEEPS // 2 - 1, pair, 0)
    for level in range(levels):
        for row in range(rows):
            out_ref[level, row] = out_ref[level, row] * inverse_ref[level, pl.ds(row, 1), :]

    for row in range(folded_rows):
        coeff_strip_ref[row] = own_coefficient_strip(coeff_ref, row)


def finish_kernel(
    owner_ref,
    pert_ref,
    interior_ref,
    strip_ref,
    coeff_strip_ref,
    from_left_ref,
    from_right_ref,
    out_ref,
    first_ref,
    second_ref,
    keep_ref,
    square_ref,
    inverse_ref,
    local_ref,
    sum_ref,
):
    members, terms, levels, rows, lanes = pert_ref.shape
    slab_rows = out_ref.shape[2]
    folded_rows, slots, packs = pack_sizes(rows)
    block = lanes // 2 // slots
    for level in range(levels):
        for pack in range(packs):
            place = level * packs + pack
            left = from_left_ref[pl.ds(place * members, members), :]
            right = from_right_ref[pl.ds(place * members, members), :]
            for slot in range(slots):
                row = pack * slots + slot
                first_ref[level, row] = joined_strip(
                    strip_ref[level, row], left, right, slot, block
                )

    strips = []
    for pack in range(packs):
        place = pl.ds(levels * (packs * members + pack), levels)
        for slot in range(slots):
            own = coeff_strip_ref[pack * slots + slot]
            strips.append(
                joined_strip(own, from_left_ref[place, :], from_right_ref[place, :], slot, block)
            )
    level_index = lax.broadcasted_iota(jnp.int32, (levels, lanes), 0)
    for row, here in enumerate(strips):
        terms_here = [
            lane_roll(here, 1),
            lane_roll(here, -1),
            jnp.where(level_index > 0, pltpu.roll(here, 1, 0), 0.0),
            jnp.where(level_index < levels - 1, pltpu.roll(here, levels - 1, 0), 0.0),
            strips[row + 1] if row < folded_rows - 1 else lane_roll(here, lanes // 2),
        ]
        if row > 0:
            terms_here.append(strips[row - 1])
        keep_ref[row] = 1.0 - here * total(terms_here)
        square_ref[row] = here * here
        inverse_ref[row] = 1.0 / jnp.where(here > 0.0, here, 1.0)

    def keep_at(level, row):
        return keep_ref[row, pl.ds(level, 1), :]

    def square_at(level, row):
        return square_ref[row, pl.ds(level, 1), :]

    def pair(index, carry):
        sweep(first_ref, second_ref, keep_at, square_at, True)
        sweep(second_ref, first_ref, keep_at, square_at, True)
        return carry

    lax.fori_loop(0, SWEEPS // 2, pair, 0)
    lane = lane_index((members, lanes))
    for level in range(levels):
        for row in range(folded_rows):
            ends = strip_ends(first_ref[level, row] * inverse_ref[row, pl.ds(level, 1), :])
            for target, end in zip((row, rows - 1 - row), ends):
                local_ref[pl.ds((level * rows + target) * members, members), :] = jnp.where(
                    (lane < SWEEPS) | (lane >= lanes - SWEEPS), end, interior_ref[level, target]
                )

    def add_level(level, carry):
        base = level * rows
        fields = [
            local_ref[pl.ds(base * members + member, rows, stride=members), :]
            for member in range(members)
        ]
        for term in range(terms):
            start = pl.multiple_of(term * levels * rows + base, rows)
            sum_ref[pl.ds(start, rows), :] = total(
                pert_ref[member, term, level].astype(jnp.float32) * fields[member]
                for member in range(members)
            )
        return carry

    lax.fori_loop(0, levels, add_level, 0)
    for slab in range(rows // slab_rows):
        owner = owner_ref[slab]
        for term in range(terms):
            for inner in range(slab_rows):
                row = slab * slab_rows + inner
                out_ref[owner, term, inner] = sum_ref[
                    pl.ds(term * levels * rows + row, levels, stride=rows), :
                ]


def whole(memory_space=pltpu.VMEM):
    return pl.BlockSpec(memory_space=memory_space)


def local_call(kernel, name, outs, scratch, operands, places, work):
    def shape_of(out):
        return out if isinstance(out, jax.ShapeDtypeStruct) else jax.ShapeDtypeStruct(out, jnp.float32)

    shapes = tuple(shape_of(out) for out in outs)
    specs = tuple(whole() for _ in outs)
    moved = sum(math.prod(x.shape) * x.dtype.itemsize for x in tuple(operands) + shapes)
    single = len(outs) == 1
    return pl.pallas_call(
        kernel,
        out_shape=shapes[0] if single else shapes,
        in_specs=[whole(place) for place in places],
        out_specs=specs[0] if single else specs,
        scratch_shapes=[
            pltpu.VMEM(item, jnp.float32) if isinstance(item, tuple) else item for item in scratch
        ],
        compiler_params=pltpu.CompilerParams(vmem_limit_bytes=VMEM_LIMIT),
        cost_estimate=pl.CostEstimate(flops=work, bytes_accessed=moved, transcendentals=0),
        name=name,
    )(*operands)


def body(perturbations, gradient_store, diffusivity, slab_owner):
    members, slots, variables, levels, rows, lanes = perturbations.shape
    terms = slots * variables
    n_member = lax.axis_size("member")
    n_tile = lax.axis_size("tile")
    slab_rows = gradient_store.shape[3]
    folded_rows, _, packs = pack_sizes(rows)
    cells = levels * rows * lanes
    wide_strip = (levels, folded_rows, members, lanes)
    strip_shape = (folded_rows, levels, lanes)
    wide_field = (levels, rows, members, lanes)
    flat_field = (levels * rows * members, lanes)
    field_coeff = (levels, rows, lanes)
    edge_shape = (levels * packs * (members + 1), lanes)
    grad_shape = (terms * levels * rows, lanes)
    vmem, smem = pltpu.VMEM, pltpu.SMEM

    pert = perturbations.reshape(members, terms, levels, rows, lanes)
    slab = gradient_store.reshape(terms, levels, slab_rows, lanes).swapaxes(1, 2)
    anchor = local_call(anchor_kernel, "anchor", [(8, lanes)], [], (), (), ANCHOR_WORK)
    gathered = lax.all_gather(slab, "member", axis=0, tiled=False)

    field, strip, to_right, to_left = local_call(
        weigh_kernel,
        "weigh",
        [flat_field, wide_strip, edge_shape, edge_shape],
        [grad_shape],
        (slab_owner, gathered, pert, diffusivity, anchor),
        (smem, vmem, vmem, vmem, vmem),
        2 * terms * members * cells,
    )
    up = [(i, i + 1) for i in range(n_tile - 1)]
    down = [(i + 1, i) for i in range(n_tile - 1)]
    from_left = lax.ppermute(to_right, "tile", up)
    from_right = lax.ppermute(to_left, "tile", down)

    interior, coeff_strip = local_call(
        interior_kernel,
        "interior",
        [wide_field, strip_shape],
        [wide_field, field_coeff, field_coeff, field_coeff],
        (field.reshape(wide_field), diffusivity),
        (vmem, vmem),
        8 * SWEEPS * members * cells,
    )
    sums = local_call(
        finish_kernel,
        "finish",
        [(n_member, terms, slab_rows, levels, lanes)],
        [wide_strip, wide_strip, strip_shape, strip_shape, strip_shape, flat_field, grad_shape],
        (slab_owner, pert, interior, strip, coeff_strip, from_left, from_right),
        (smem,) + (vmem,) * 6,
        2 * terms * members * cells,
    )
    received = lax.all_to_all(sums, "member", 0, 0, tiled=True)
    norm_factor = 1.0 / (members * n_member - 1)
    owned = jnp.sum(received, axis=0) * norm_factor
    return owned.swapaxes(1, 2).reshape(slots, variables, levels, slab_rows, lanes)


def solution(mesh):
    in_specs = (
        P("member", None, None, None, None, "tile"),
        P(None, None, None, "member", "tile"),
        P(None, None, "tile"),
        P(),
    )
    out_specs = P(None, None, None, "member", "tile")
    return jax.shard_map(body, mesh=mesh, in_specs=in_specs, out_specs=out_specs, check_vma=False)
```

profile of v0, /device:TPU:0, one launch (start us, length us, event | category | flops | bytes accessed | tf_op | source)
XLA Modules:
  0.0 35.9 jit_solution(2179179974868832574)
XLA Ops:
  0.0 0.0 copy-start.3
  0.0 0.0 copy-start.2
  0.0 0.0 copy-start.1
  0.0 0.0 copy-start
  0.0 0.8 %copy-done.3 = f32[2,5,8,1,128]{4,3,2,1,0:T(1,128)S(1)} copy-done((f32[2,5,8,1,128]{4,3,2,1,0:T(1,128)S(1)}, f32[2,5,8,1,128]{4,3,2,1,0:T(1,128)}, u32[]{:S(2)}) %copy-start.3) | copy-done | bytes 40984
  0.8 10.9 %all_gather.3.gathered_ref = f32[8,10,1,8,128]{4,3,2,1,0:T(8,128)S(1)} all-gather(f32[1,10,1,8,128]{4,3,2,1,0:T(8,128)S(1)} %bitcast.7), channel_id=1, replica_groups=mesh['member'=8,'tile'=4] {'member'}, dimensions={0}, use_global_device_ids=true | all-gather | bytes 368640 | tf_op jit(solution)/shard_map/all_gather | solution.py:397
  11.7 0.0 copy-done.2
  11.7 0.0 copy-done.1
  11.7 0.0 copy-done
  11.7 1.5 %weigh.1 = (f32[512,128]{1,0:T(8,128)S(1)}, f32[8,4,8,128]{3,2,1,0:T(8,128)S(1)}, f32[72,128]{1,0:T(8,128)S(1)}, f32[72,128]{1,0:T(8,128)S(1)}) custom-call(s32[8]{0:T(128)S(1)} %copy-done.2, f32[8,10,1,8,128]{4,3,2,1,0:T(8,128)S(1)} %all_gather.3.gathered_ref, bf16[8,10,8,8,128]{4,3,2,1,0:T(8,128)(2,1)S(1)} %bitcast.4, f32[8,8,128]{2,1,0:T(8,128)S(1)} %copy-done.1, ...), custom_call_target="tpu_custom_call" | custom-call | flops 1310720 | bytes 2142240 | tf_op jit(solution)/shard_map/weigh/pallas_call | solution.py:363
  13.2 3.5 %collective-permute-start = (f32[72,128]{1,0:T(8,128)S(1)}, f32[72,128]{1,0:T(8,128)S(1)}, u32[]{:S(2)}, u32[]{:S(2)}) collective-permute-start(f32[72,128]{1,0:T(8,128)S(1)} %get-tuple-element.15), channel_id=1, source_target_pairs={{0,1},{1,2},{2,3},{4,5},{5,6},{6,7},{8,9},{9,10},{10,11},{12,13},{... | collective-permute-start | bytes 110600 | tf_op jit(solution)/shard_map/ppermute | solution.py:410
  16.7 1.3 %collective-permute-start.1 = (f32[72,128]{1,0:T(8,128)S(1)}, f32[72,128]{1,0:T(8,128)S(1)}, u32[]{:S(2)}, u32[]{:S(2)}) collective-permute-start(f32[72,128]{1,0:T(8,128)S(1)} %get-tuple-element.16), channel_id=1, source_target_pairs={{1,0},{2,1},{3,2},{5,4},{6,5},{7,6},{9,8},{10,9},{11,10},{13,12},{... | collective-permute-start | bytes 110600 | tf_op jit(solution)/shard_map/ppermute | solution.py:411
  18.0 1.9 %interior.1 = (f32[8,8,8,128]{3,2,1,0:T(8,128)S(1)}, f32[4,8,128]{2,1,0:T(8,128)S(1)}) custom-call(f32[8,8,8,128]{3,2,1,0:T(8,128)S(1)} %bitcast.6, f32[8,8,128]{2,1,0:T(8,128)S(1)} %copy-done.1), custom_call_target="tpu_custom_call" | custom-call | flops 5242880 | bytes 573440 | tf_op jit(solution)/shard_map/interior/pallas_call | solution.py:363
  19.9 0.0 collective-permute-done.from_left_ref
  19.9 2.7 %collective-permute-done.1.from_right_ref = f32[72,128]{1,0:T(8,128)S(1)} collective-permute-done((f32[72,128]{1,0:T(8,128)S(1)}, f32[72,128]{1,0:T(8,128)S(1)}, u32[]{:S(2)}, u32[]{:S(2)}) %collective-permute-start.1) | collective-permute-done | bytes 36896 | tf_op jit(solution)/shard_map/ppermute | solution.py:411
  22.6 2.5 %finish.1 = f32[8,10,1,8,128]{4,3,2,1,0:T(8,128)S(1)} custom-call(s32[8]{0:T(128)S(1)} %copy-done.2, bf16[8,10,8,8,128]{4,3,2,1,0:T(8,128)(2,1)S(1)} %bitcast.5, f32[8,8,8,128]{3,2,1,0:T(8,128)S(1)} %get-tuple-element.12.interior_ref, f32[8,4,8,128]{3,2,1,0:T(8,128)S(1)} %get-tuple-element.13.strip_ref, f32[4,8,128]{2,1,0:T(8,128)S(1)} %get-tuple-element.14.coeff_strip_ref, ...), custom_call_target="tpu_custom_call" | custom-call | flops 1310720 | bytes 2121760 | tf_op jit(solution)/shard_map/finish/pallas_call | solution.py:363
  25.1 10.2 %all_to_all.5 = f32[8,10,1,8,128]{4,3,2,1,0:T(8,128)S(1)} all-to-all(f32[8,10,1,8,128]{4,3,2,1,0:T(8,128)S(1)} %finish.1), channel_id=1, replica_groups=mesh['member'=8,'tile'=4] {'member'}, dimensions={0} | all-to-all | bytes 655360 | tf_op jit(solution)/shard_map/all_to_all | solution.py:431
  35.3 0.6 %broadcast_multiply_fusion = f32[10,8,128]{2,1,0:T(8,128)} fusion(f32[10,8,128]{2,1,0:T(8,128)S(1)} %reduce_sum.9), kind=kLoop, calls=%fused_computation | loop fusion | flops 10240 | bytes 81920 | tf_op jit(solution)/shard_map/mul | solution.py:433
  (2 shorter events, 0.0 us)
Async XLA Ops:
  0.0 0.8 %copy-start.3 = (f32[2,5,8,1,128]{4,3,2,1,0:T(1,128)S(1)}, f32[2,5,8,1,128]{4,3,2,1,0:T(1,128)}, u32[]{:S(2)}) copy-start(f32[2,5,8,1,128]{4,3,2,1,0:T(1,128)} %param.5) | copy-start | bytes 122884
  0.0 11.7 %copy-start.2 = (s32[8]{0:T(128)S(1)}, s32[8]{0:T(128)}, u32[]{:S(2)}) copy-start(s32[8]{0:T(128)} %owner_ref.3) | copy-start | bytes 100
  0.0 11.7 %copy-start.1 = (f32[8,8,128]{2,1,0:T(8,128)S(1)}, f32[8,8,128]{2,1,0:T(8,128)}, u32[]{:S(2)}) copy-start(f32[8,8,128]{2,1,0:T(8,128)} %coeff_ref.3) | copy-start | bytes 98308
  0.0 11.7 %copy-start = (bf16[8,2,5,8,8,128]{5,4,3,2,1,0:T(8,128)(2,1)S(1)}, bf16[8,2,5,8,8,128]{5,4,3,2,1,0:T(8,128)(2,1)}, u32[]{:S(2)}) copy-start(bf16[8,2,5,8,8,128]{5,4,3,2,1,0:T(8,128)(2,1)} %param.4) | copy-start | bytes 3932164
  13.2 6.7 %collective-permute-start = (f32[72,128]{1,0:T(8,128)S(1)}, f32[72,128]{1,0:T(8,128)S(1)}, u32[]{:S(2)}, u32[]{:S(2)}) collective-permute-start(f32[72,128]{1,0:T(8,128)S(1)} %get-tuple-element.15), channel_id=1, source_target_pairs={{0,1},{1,2},{2,3},{4,5},{5,6},{6,7},{8,9},{9,10},{10,11},{12,13},{... | collective-permute-start | bytes 110600 | tf_op jit(solution)/shard_map/ppermute | solution.py:410
  16.7 5.9 %collective-permute-start.1 = (f32[72,128]{1,0:T(8,128)S(1)}, f32[72,128]{1,0:T(8,128)S(1)}, u32[]{:S(2)}, u32[]{:S(2)}) collective-permute-start(f32[72,128]{1,0:T(8,128)S(1)} %get-tuple-element.16), channel_id=1, source_target_pairs={{1,0},{2,1},{3,2},{5,4},{6,5},{7,6},{9,8},{10,9},{11,10},{13,12},{... | collective-permute-start | bytes 110600 | tf_op jit(solution)/shard_map/ppermute | solution.py:411
where the time goes:
time: 36.2 us; the launch traced here: 35.9 us
  blocking collectives  21.1 us (58%)
  Pallas kernels  5.91 us (16%)
  starting transfers between devices  4.79 us (13%)
  waiting for transfers between devices  2.69 us (7%)
  local copies, waits for them, and re-layouts  0.78 us (2%)
  other arithmetic  0.64 us (2%)
    all_gather x1, blocking collectives, body(): gathered = lax.all_gather(slab, 'member', axis=0, tiled=False)  10.9 us
    all_to_all x1, blocking collectives, body(): received = lax.all_to_all(sums, 'member', 0, 0, tiled=True)  10.2 us
    pallas_call x4, Pallas kernels, local_call(): pl.pallas_call(kernel, out_shape=shapes[0] if single else shapes, in_spec...  5.91 us
    ppermute x1, starting transfers between devices, body(): from_left = lax.ppermute(to_right, 'tile', up)  3.5 us
    ppermute x1, waiting for transfers between devices, body(): from_right = lax.ppermute(to_left, 'tile', down)  2.69 us
    ppermute x1, starting transfers between devices, body(): from_right = lax.ppermute(to_left, 'tile', down)  1.29 us
    unnamed x8, local copies, waits for them, and re-layouts  0.78 us
  transfers between devices with their start and end apart: 2, of which 1 were waited for; matrix products, arithmetic and copies ran while one was open for 0% of the time, Pallas kernels for 5%

commit v1 on v0

v1 whole, which is shorter than its diff:
```python
import math

import jax
import jax.numpy as jnp
from jax import lax
from jax.experimental import pallas as pl
from jax.experimental.pallas import tpu as pltpu
from jax.sharding import PartitionSpec as P

SWEEPS = 10
GROUPS = 4
ANCHOR_WORK = 10**10
VMEM_LIMIT = 16 * 1024 * 1024


def lane_roll(value, shift):
    shift = shift % value.shape[-1]
    return value if shift == 0 else pltpu.roll(value, shift, 1)


def lane_index(shape):
    return lax.broadcasted_iota(jnp.int32, shape, 1)


def spread(row, rows=8):
    return jnp.broadcast_to(row, (rows, row.shape[-1]))


def whole(memory_space=pltpu.VMEM):
    return pl.BlockSpec(memory_space=memory_space)


def mirrors(level, row, levels, rows):
    return [
        (far_level, far_row)
        for far_level in (level, levels - 1 - level)
        for far_row in (row, rows - 1 - row)
    ]


def group_index(shape, start):
    part = shape[-1] // GROUPS
    return (lane_index(shape) + start) % shape[-1] // part


def own_strips(values):
    part = values[0].shape[-1] // GROUPS
    rolled = [lane_roll(value, part * g) for g, value in enumerate(values)]
    both = []
    for start in (SWEEPS, part - SWEEPS):
        group = group_index(values[0].shape, start)
        strip = rolled[0]
        for g in range(1, GROUPS):
            strip = jnp.where(group == g, rolled[g], strip)
        both.append(strip)
    return both


def packed_edges(first, second):
    part = first.shape[-1] // GROUPS
    place = lane_index(first.shape) % part
    moved = lane_roll(second, part // 2)
    to_right = jnp.where(place >= part // 2, first, moved)
    to_left = jnp.where(place < part // 2, first, moved)
    return to_right, to_left


def joined_strip(own, edge, index, is_left):
    part = own.shape[-1] // GROUPS
    place = lane_index(own.shape) % part
    edge = lane_roll(edge, -(index % 2) * (part // 2))
    return jnp.where(place >= part - SWEEPS if is_left else place < SWEEPS, edge, own)


def row_mirrored(value, start):
    part = value.shape[-1] // GROUPS
    group = group_index(value.shape, start)
    return jnp.where(group % 2 == 0, lane_roll(value, -part), lane_roll(value, part))


def total(terms):
    terms = list(terms)
    while len(terms) > 1:
        terms = [
            terms[i] + terms[i + 1] if i + 1 < len(terms) else terms[i]
            for i in range(0, len(terms), 2)
        ]
    return terms[0]


def around(planes, level, row, start=None):
    levels, rows = len(planes), len(planes[level])
    here = planes[level][row]
    terms = [lane_roll(here, 1), lane_roll(here, -1)]
    if row > 0:
        terms.append(planes[level][row - 1])
    if row < rows - 1:
        terms.append(planes[level][row + 1])
    elif start is not None:
        terms.append(row_mirrored(here, start))
    if level > 0:
        terms.append(planes[level - 1][row])
    if level < levels - 1:
        terms.append(planes[level + 1][row])
    elif start is not None:
        terms.append(lane_roll(here, here.shape[-1] // 2))
    return total(terms)


def sweep(source, target, keep_at, square_at, start=None):
    levels, rows = source.shape[0], source.shape[1]
    planes = [[source[level, row] for row in range(rows)] for level in range(levels)]
    for level in range(levels):
        for row in range(rows):
            target[level, row] = keep_at(level, row) * planes[level][row] + square_at(
                level, row
            ) * around(planes, level, row, start)


def anchor_kernel(out_ref):
    out_ref[...] = jnp.zeros_like(out_ref)


def weigh_kernel(
    owner_ref,
    gathered_ref,
    pert_ref,
    coeff_ref,
    anchor_ref,
    field_ref,
    left_ref,
    right_ref,
    coeff_left_ref,
    coeff_right_ref,
    to_right_ref,
    to_left_ref,
    grad_ref,
):
    members, terms, levels, rows, lanes = pert_ref.shape
    slab_rows = gathered_ref.shape[2]
    strip_levels, strip_rows = left_ref.shape[:2]
    for slab in range(rows // slab_rows):
        owner = owner_ref[slab]
        for term in range(terms):
            for inner in range(slab_rows):
                row = slab * slab_rows + inner
                grad_ref[pl.ds(term * levels * rows + row, levels, stride=rows), :] = gathered_ref[
                    owner, term, inner
                ]

    def weigh_level(level, carry):
        base = level * rows
        coeff = coeff_ref[level]
        gradients = [
            coeff * grad_ref[pl.ds(pl.multiple_of(term * levels * rows + base, rows), rows), :]
            for term in range(terms)
        ]
        for member in range(members):
            field_ref[pl.ds(base * members + member, rows, stride=members), :] = total(
                pert_ref[member, term, level].astype(jnp.float32) * gradients[term]
                for term in range(terms)
            )
        return carry

    lax.fori_loop(0, levels, weigh_level, 0)

    pairs = strip_levels * strip_rows // 2
    fields, coeffs = [], []
    for level in range(strip_levels):
        for row in range(strip_rows):
            index = level * strip_rows + row
            cells = mirrors(level, row, levels, rows)
            field = own_strips(
                [field_ref[pl.ds((l * rows + r) * members, members), :] for l, r in cells]
            )
            coeff = own_strips([spread(coeff_ref[l, pl.ds(r, 1), :]) for l, r in cells])
            left_ref[level, row], right_ref[level, row] = field
            coeff_left_ref[pl.ds(index, 1), :] = coeff[0][0:1]
            coeff_right_ref[pl.ds(index, 1), :] = coeff[1][0:1]
            fields.append(field[0])
            coeffs.append(coeff[0])
    for pair in range(pairs):
        edges = packed_edges(fields[2 * pair], fields[2 * pair + 1])
        coeff_edges = packed_edges(coeffs[2 * pair], coeffs[2 * pair + 1])
        for ref, edge, coeff_edge in zip((to_right_ref, to_left_ref), edges, coeff_edges):
            ref[pl.ds(pair * members, members), :] = edge
            ref[pl.ds(pairs * members + pair, 1), :] = coeff_edge[0:1]


def interior_kernel(field_ref, coeff_ref, out_ref, other_ref, keep_ref, square_ref, inverse_ref):
    levels, rows, members, lanes = field_ref.shape
    row_index = lax.broadcasted_iota(jnp.int32, (rows, lanes), 0)
    for level in range(levels):
        here = coeff_ref[level]
        terms = [
            lane_roll(here, 1),
            lane_roll(here, -1),
            jnp.where(row_index > 0, pltpu.roll(here, 1, 0), 0.0),
            jnp.where(row_index < rows - 1, pltpu.roll(here, rows - 1, 0), 0.0),
        ]
        if level > 0:
            terms.append(coeff_ref[level - 1])
        if level < levels - 1:
            terms.append(coeff_ref[level + 1])
        keep_ref[level] = 1.0 - here * total(terms)
        square_ref[level] = here * here
        inverse_ref[level] = 1.0 / here

    def keep_at(level, row):
        return keep_ref[level, pl.ds(row, 1), :]

    def square_at(level, row):
        return square_ref[level, pl.ds(row, 1), :]

    sweep(field_ref, other_ref, keep_at, square_at)
    sweep(other_ref, out_ref, keep_at, square_at)

    def pair(index, carry):
        sweep(out_ref, other_ref, keep_at, square_at)
        sweep(other_ref, out_ref, keep_at, square_at)
        return carry

    lax.fori_loop(0, SWEEPS // 2 - 1, pair, 0)
    for level in range(levels):
        for row in range(rows):
            out_ref[level, row] = out_ref[level, row] * inverse_ref[level, pl.ds(row, 1), :]


def swept_ends(
    strip_ref, coeff_ref, edge_ref, levels, rows, is_left, put, first_ref, second_ref, keep_ref, square_ref
):
    strip_levels, strip_rows, members, lanes = strip_ref.shape
    part = lanes // GROUPS
    start = SWEEPS if is_left else part - SWEEPS
    pairs = strip_levels * strip_rows // 2
    coeffs = []
    for level in range(strip_levels):
        plane = []
        for row in range(strip_rows):
            index = level * strip_rows + row
            edge = edge_ref[pl.ds(index // 2 * members, members), :]
            coeff_edge = spread(edge_ref[pl.ds(pairs * members + index // 2, 1), :])
            first_ref[level, row] = joined_strip(strip_ref[level, row], edge, index, is_left)
            plane.append(
                joined_strip(spread(coeff_ref[pl.ds(index, 1), :]), coeff_edge, index, is_left)
            )
        coeffs.append(plane)
    for level in range(strip_levels):
        for row in range(strip_rows):
            here = coeffs[level][row]
            keep_ref[level, row] = 1.0 - here * around(coeffs, level, row, start)
            square_ref[level, row] = here * here

    def keep_at(level, row):
        return keep_ref[level, row]

    def square_at(level, row):
        return square_ref[level, row]

    def pair(index, carry):
        sweep(first_ref, second_ref, keep_at, square_at, start)
        sweep(second_ref, first_ref, keep_at, square_at, start)
        return carry

    lax.fori_loop(0, SWEEPS // 2, pair, 0)
    for level in range(strip_levels):
        for row in range(strip_rows):
            coeff = spread(coeff_ref[pl.ds(level * strip_rows + row, 1), :])
            final = first_ref[level, row] / jnp.where(coeff > 0.0, coeff, 1.0)
            for g, (l, r) in enumerate(mirrors(level, row, levels, rows)):
                put(l, r, lane_roll(final, -part * g))


def left_kernel(interior_ref, strip_ref, coeff_ref, edge_ref, out_ref, *scratch):
    levels, rows, members, lanes = interior_ref.shape
    lane = lane_index((members, lanes))

    def put(level, row, end):
        out_ref[level, row] = jnp.where(lane < SWEEPS, end, interior_ref[level, row])

    swept_ends(strip_ref, coeff_ref, edge_ref, levels, rows, True, put, *scratch)


def finish_kernel(
    owner_ref,
    pert_ref,
    partial_ref,
    strip_ref,
    coeff_ref,
    edge_ref,
    out_ref,
    local_ref,
    sum_ref,
    *scratch,
):
    members, terms, levels, rows, lanes = pert_ref.shape
    slab_rows = out_ref.shape[2]
    lane = lane_index((members, lanes))

    def put(level, row, end):
        local_ref[pl.ds((level * rows + row) * members, members), :] = jnp.where(
            lane >= lanes - SWEEPS, end, partial_ref[level, row]
        )

    swept_ends(strip_ref, coeff_ref, edge_ref, levels, rows, False, put, *scratch)

    def add_level(level, carry):
        base = level * rows
        fields = [
            local_ref[pl.ds(base * members + member, rows, stride=members), :]
            for member in range(members)
        ]
        for term in range(terms):
            start = pl.multiple_of(term * levels * rows + base, rows)
            sum_ref[pl.ds(start, rows), :] = total(
                pert_ref[member, term, level].astype(jnp.float32) * fields[member]
                for member in range(members)
            )
        return carry

    lax.fori_loop(0, levels, add_level, 0)
    for slab in range(rows // slab_rows):
        owner = owner_ref[slab]
        for term in range(terms):
            for inner in range(slab_rows):
                row = slab * slab_rows + inner
                out_ref[owner, term, inner] = sum_ref[
                    pl.ds(term * levels * rows + row, levels, stride=rows), :
                ]


def local_call(kernel, name, outs, scratch, operands, places, work):
    def shape_of(out):
        return out if isinstance(out, jax.ShapeDtypeStruct) else jax.ShapeDtypeStruct(out, jnp.float32)

    shapes = tuple(shape_of(out) for out in outs)
    specs = tuple(whole() for _ in outs)
    moved = sum(math.prod(x.shape) * x.dtype.itemsize for x in tuple(operands) + shapes)
    single = len(outs) == 1
    return pl.pallas_call(
        kernel,
        out_shape=shapes[0] if single else shapes,
        in_specs=[whole(place) for place in places],
        out_specs=specs[0] if single else specs,
        scratch_shapes=[
            pltpu.VMEM(item, jnp.float32) if isinstance(item, tuple) else item for item in scratch
        ],
        compiler_params=pltpu.CompilerParams(vmem_limit_bytes=VMEM_LIMIT),
        cost_estimate=pl.CostEstimate(flops=work, bytes_accessed=moved, transcendentals=0),
        name=name,
    )(*operands)


def body(perturbations, gradient_store, diffusivity, slab_owner):
    members, slots, variables, levels, rows, lanes = perturbations.shape
    terms = slots * variables
    n_member = lax.axis_size("member")
    n_tile = lax.axis_size("tile")
    slab_rows = gradient_store.shape[3]
    cells = levels * rows * lanes
    strip_levels, strip_rows = levels // 2, rows // 2
    strips = strip_levels * strip_rows
    wide_strip = (strip_levels, strip_rows, members, lanes)
    coeff_wide_strip = (strip_levels, strip_rows, 8, lanes)
    strip_scratch = [wide_strip, wide_strip, coeff_wide_strip, coeff_wide_strip]
    coeff_strip = (strips, lanes)
    wide_field = (levels, rows, members, lanes)
    flat_field = (levels * rows * members, lanes)
    field_coeff = (levels, rows, lanes)
    edge_shape = (strips // 2 * (members + 1), lanes)
    grad_shape = (terms * levels * rows, lanes)
    vmem, smem = pltpu.VMEM, pltpu.SMEM

    pert = perturbations.reshape(members, terms, levels, rows, lanes)
    slab = gradient_store.reshape(terms, levels, slab_rows, lanes).swapaxes(1, 2)
    anchor = local_call(anchor_kernel, "anchor", [(8, lanes)], [], (), (), ANCHOR_WORK)
    gathered = lax.all_gather(slab, "member", axis=0, tiled=False)

    field, left, right, coeff_left, coeff_right, to_right, to_left = local_call(
        weigh_kernel,
        "weigh",
        [flat_field, wide_strip, wide_strip, coeff_strip, coeff_strip, edge_shape, edge_shape],
        [grad_shape],
        (slab_owner, gathered, pert, diffusivity, anchor),
        (smem, vmem, vmem, vmem, vmem),
        2 * terms * members * cells,
    )
    up = [(i, i + 1) for i in range(n_tile - 1)]
    down = [(i + 1, i) for i in range(n_tile - 1)]
    from_left = lax.ppermute(to_right, "tile", up)
    from_right = lax.ppermute(to_left, "tile", down)

    interior = local_call(
        interior_kernel,
        "interior",
        [wide_field],
        [wide_field, field_coeff, field_coeff, field_coeff],
        (field.reshape(wide_field), diffusivity),
        (vmem, vmem),
        8 * SWEEPS * members * cells,
    )
    partial = local_call(
        left_kernel,
        "left_strips",
        [wide_field],
        strip_scratch,
        (interior, left, coeff_left, from_left),
        (vmem,) * 4,
        2 * SWEEPS * members * cells,
    )
    sums = local_call(
        finish_kernel,
        "finish",
        [(n_member, terms, slab_rows, levels, lanes)],
        [flat_field, grad_shape] + strip_scratch,
        (slab_owner, pert, partial, right, coeff_right, from_right),
        (smem,) + (vmem,) * 5,
        2 * terms * members * cells,
    )
    received = lax.all_to_all(sums, "member", 0, 0, tiled=True)
    norm_factor = 1.0 / (members * n_member - 1)
    owned = jnp.sum(received, axis=0) * norm_factor
    return owned.swapaxes(1, 2).reshape(slots, variables, levels, slab_rows, lanes)


def solution(mesh):
    in_specs = (
        P("member", None, None, None, None, "tile"),
        P(None, None, None, "member", "tile"),
        P(None, None, "tile"),
        P(),
    )
    out_specs = P(None, None, None, "member", "tile")
    return jax.shard_map(body, mesh=mesh, in_specs=in_specs, out_specs=out_specs, check_vma=False)
```

time: 36.2 us -> 35.8 us (0.989)
  waiting for transfers between devices: 2.69 us -> 1.42 us
  Pallas kernels: 5.91 us -> 6.76 us
    ppermute x1, waiting for transfers between devices: 2.69 us -> 1.41 us  [body(): from_right = lax.ppermute(to_left, 'tile', down)]
    pallas_call x4 -> x5, Pallas kernels: 5.91 us -> 6.76 us  [local_call(): pl.pallas_call(kernel, out_shape=shapes[0] if single else shapes, in_spec...]
  transfers between devices with their start and end apart: 2 -> 2, of which waited for: 1 -> 1; matrix products, arithmetic and copies ran while one was open for 0% -> 0% of each run, Pallas kernels for 5% -> 9%
where the time goes in v1:
time: 35.8 us; the launch traced here: 35.5 us
  blocking collectives  21.1 us (59%)
  Pallas kernels  6.76 us (19%)
  starting transfers between devices  4.79 us (13%)
  waiting for transfers between devices  1.42 us (4%)
  local copies, waits for them, and re-layouts  0.78 us (2%)
  other arithmetic  0.64 us (2%)
    all_gather x1, blocking collectives, body(): gathered = lax.all_gather(slab, 'member', axis=0, tiled=False)  10.9 us
    all_to_all x1, blocking collectives, body(): received = lax.all_to_all(sums, 'member', 0, 0, tiled=True)  10.2 us
    pallas_call x5, Pallas kernels, local_call(): pl.pallas_call(kernel, out_shape=shapes[0] if single else shapes, in_spec...  6.76 us
    ppermute x1, starting transfers between devices, body(): from_left = lax.ppermute(to_right, 'tile', up)  3.5 us
    ppermute x1, waiting for transfers between devices, body(): from_right = lax.ppermute(to_left, 'tile', down)  1.41 us
    ppermute x1, starting transfers between devices, body(): from_right = lax.ppermute(to_left, 'tile', down)  1.29 us
    unnamed x8, local copies, waits for them, and re-layouts  0.78 us
  transfers between devices with their start and end apart: 2, of which 1 were waited for; matrix products, arithmetic and copies ran while one was open for 0% of the time, Pallas kernels for 9%

profile of v1, /device:TPU:0, one launch (start us, length us, event | category | flops | bytes accessed | tf_op | source)
XLA Modules:
  0.0 35.5 jit_solution(13168128884265617846)
XLA Ops:
  0.0 0.0 copy-start.3
  0.0 0.0 copy-start.2
  0.0 0.0 copy-start.1
  0.0 0.0 copy-start
  0.0 0.8 %copy-done.3 = f32[2,5,8,1,128]{4,3,2,1,0:T(1,128)S(1)} copy-done((f32[2,5,8,1,128]{4,3,2,1,0:T(1,128)S(1)}, f32[2,5,8,1,128]{4,3,2,1,0:T(1,128)}, u32[]{:S(2)}) %copy-start.3) | copy-done | bytes 40984
  0.8 10.9 %all_gather.3.gathered_ref = f32[8,10,1,8,128]{4,3,2,1,0:T(8,128)S(1)} all-gather(f32[1,10,1,8,128]{4,3,2,1,0:T(8,128)S(1)} %bitcast.7), channel_id=1, replica_groups=mesh['member'=8,'tile'=4] {'member'}, dimensions={0}, use_global_device_ids=true | all-gather | bytes 368640 | tf_op jit(solution)/shard_map/all_gather | solution.py:377
  11.7 0.0 copy-done.2
  11.7 0.0 copy-done.1
  11.7 0.0 copy-done
  11.7 1.3 %weigh.1 = (f32[512,128]{1,0:T(8,128)S(1)}, f32[4,4,8,128]{3,2,1,0:T(8,128)S(1)}, f32[4,4,8,128]{3,2,1,0:T(8,128)S(1)}, f32[16,128]{1,0:T(8,128)S(1)}, f32[16,12...) custom-call(s32[8]{0:T(128)S(1)} %copy-done.2, f32[8,10,1,8,128]{4,3,2,1,0:T(8,128)S(1)} %all_gather.3.gathered_ref, ...), custom_call_target="tpu_custom_call" | custom-call | flops 1310720 | bytes 2158624 | tf_op jit(solution)/shard_map/weigh/pallas_call | solution.py:340
  13.0 3.5 %collective-permute-start = (f32[72,128]{1,0:T(8,128)S(1)}, f32[72,128]{1,0:T(8,128)S(1)}, u32[]{:S(2)}, u32[]{:S(2)}) collective-permute-start(f32[72,128]{1,0:T(8,128)S(1)} %get-tuple-element.15), channel_id=1, source_target_pairs={{0,1},{1,2},{2,3},{4,5},{5,6},{6,7},{8,9},{9,10},{10,11},{12,13},{... | collective-permute-start | bytes 110600 | tf_op jit(solution)/shard_map/ppermute | solution.py:390
  16.5 1.3 %collective-permute-start.1 = (f32[72,128]{1,0:T(8,128)S(1)}, f32[72,128]{1,0:T(8,128)S(1)}, u32[]{:S(2)}, u32[]{:S(2)}) collective-permute-start(f32[72,128]{1,0:T(8,128)S(1)} %get-tuple-element.18), channel_id=1, source_target_pairs={{1,0},{2,1},{3,2},{5,4},{6,5},{7,6},{9,8},{10,9},{11,10},{13,12},{... | collective-permute-start | bytes 110600 | tf_op jit(solution)/shard_map/ppermute | solution.py:391
  17.8 1.8 %interior.1.interior_ref = f32[8,8,8,128]{3,2,1,0:T(8,128)S(1)} custom-call(f32[8,8,8,128]{3,2,1,0:T(8,128)S(1)} %bitcast.6, f32[8,8,128]{2,1,0:T(8,128)S(1)} %copy-done.1), custom_call_target="tpu_custom_call" | custom-call | flops 5242880 | bytes 557056 | tf_op jit(solution)/shard_map/interior/pallas_call | solution.py:340
  19.5 0.0 collective-permute-done.edge_ref
  19.6 1.3 %left_strips.1.partial_ref = f32[8,8,8,128]{3,2,1,0:T(8,128)S(1)} custom-call(f32[8,8,8,128]{3,2,1,0:T(8,128)S(1)} %interior.1.interior_ref, f32[4,4,8,128]{3,2,1,0:T(8,128)S(1)} %get-tuple-element.13.strip_ref, f32[16,128]{1,0:T(8,128)S(1)} %get-tuple-element.14.coeff_ref, f32[72,128]{1,0:T(8,128)S(1)} %collective-permute-done.edge_ref), custom_call_target="tpu_custom_call" | custom-call | flops 1310720 | bytes 634880 | tf_op jit(solution)/shard_map/left_strips/pallas_call | solution.py:340
  20.9 1.4 %collective-permute-done.1.edge_ref = f32[72,128]{1,0:T(8,128)S(1)} collective-permute-done((f32[72,128]{1,0:T(8,128)S(1)}, f32[72,128]{1,0:T(8,128)S(1)}, u32[]{:S(2)}, u32[]{:S(2)}) %collective-permute-start.1) | collective-permute-done | bytes 36896 | tf_op jit(solution)/shard_map/ppermute | solution.py:391
  22.3 2.4 %finish.1 = f32[8,10,1,8,128]{4,3,2,1,0:T(8,128)S(1)} custom-call(s32[8]{0:T(128)S(1)} %copy-done.2, bf16[8,10,8,8,128]{4,3,2,1,0:T(8,128)(2,1)S(1)} %bitcast.5, f32[8,8,8,128]{3,2,1,0:T(8,128)S(1)} %left_strips.1.partial_ref, f32[4,4,8,128]{3,2,1,0:T(8,128)S(1)} %get-tuple-element.16.strip_ref, f32[16,128]{1,0:T(8,128)S(1)} %get-tuple-element.17.coeff_ref, ...), custom_call_target="tpu_custom_call" | custom-call | flops 1310720 | bytes 2011168 | tf_op jit(solution)/shard_map/finish/pallas_call | solution.py:340
  24.7 10.2 %all_to_all.5 = f32[8,10,1,8,128]{4,3,2,1,0:T(8,128)S(1)} all-to-all(f32[8,10,1,8,128]{4,3,2,1,0:T(8,128)S(1)} %finish.1), channel_id=1, replica_groups=mesh['member'=8,'tile'=4] {'member'}, dimensions={0} | all-to-all | bytes 655360 | tf_op jit(solution)/shard_map/all_to_all | solution.py:420
  34.9 0.6 %broadcast_multiply_fusion = f32[10,8,128]{2,1,0:T(8,128)} fusion(f32[10,8,128]{2,1,0:T(8,128)S(1)} %reduce_sum.9), kind=kLoop, calls=%fused_computation | loop fusion | flops 10240 | bytes 81920 | tf_op jit(solution)/shard_map/mul | solution.py:422
  (2 shorter events, 0.0 us)
Async XLA Ops:
  0.0 0.8 %copy-start.3 = (f32[2,5,8,1,128]{4,3,2,1,0:T(1,128)S(1)}, f32[2,5,8,1,128]{4,3,2,1,0:T(1,128)}, u32[]{:S(2)}) copy-start(f32[2,5,8,1,128]{4,3,2,1,0:T(1,128)} %param.5) | copy-start | bytes 122884
  0.0 11.7 %copy-start.2 = (s32[8]{0:T(128)S(1)}, s32[8]{0:T(128)}, u32[]{:S(2)}) copy-start(s32[8]{0:T(128)} %owner_ref.3) | copy-start | bytes 100
  0.0 11.7 %copy-start.1 = (f32[8,8,128]{2,1,0:T(8,128)S(1)}, f32[8,8,128]{2,1,0:T(8,128)}, u32[]{:S(2)}) copy-start(f32[8,8,128]{2,1,0:T(8,128)} %coeff_ref.3) | copy-start | bytes 98308
  0.0 11.7 %copy-start = (bf16[8,2,5,8,8,128]{5,4,3,2,1,0:T(8,128)(2,1)S(1)}, bf16[8,2,5,8,8,128]{5,4,3,2,1,0:T(8,128)(2,1)}, u32[]{:S(2)}) copy-start(bf16[8,2,5,8,8,128]{5,4,3,2,1,0:T(8,128)(2,1)} %param.4) | copy-start | bytes 3932164
  13.0 6.6 %collective-permute-start = (f32[72,128]{1,0:T(8,128)S(1)}, f32[72,128]{1,0:T(8,128)S(1)}, u32[]{:S(2)}, u32[]{:S(2)}) collective-permute-start(f32[72,128]{1,0:T(8,128)S(1)} %get-tuple-element.15), channel_id=1, source_target_pairs={{0,1},{1,2},{2,3},{4,5},{5,6},{6,7},{8,9},{9,10},{10,11},{12,13},{... | collective-permute-start | bytes 110600 | tf_op jit(solution)/shard_map/ppermute | solution.py:390
  16.5 5.9 %collective-permute-start.1 = (f32[72,128]{1,0:T(8,128)S(1)}, f32[72,128]{1,0:T(8,128)S(1)}, u32[]{:S(2)}, u32[]{:S(2)}) collective-permute-start(f32[72,128]{1,0:T(8,128)S(1)} %get-tuple-element.18), channel_id=1, source_target_pairs={{1,0},{2,1},{3,2},{5,4},{6,5},{7,6},{9,8},{10,9},{11,10},{13,12},{... | collective-permute-start | bytes 110600 | tf_op jit(solution)/shard_map/ppermute | solution.py:391
